TPU v7x, 768 devices: a whole 4x8x12 slice. The times are simulated.
768 devices in a mesh: blk: 384 (over z, y_lo, x, core), grp: 2 (over y_hi).
Axes of the slice: x: 4, y: 8 (y_hi: 2, y_lo: 4; y = y_hi * 4 + y_lo), z: 12, core: 2. Of those that a mesh axis runs over, the one named last changes fastest.
Arguments:
- image_embed: bfloat16 [98304, 1152], P(('blk', 'grp')), may hold values from -6 to 6
- text_embed: bfloat16 [98304, 1152], P(('blk', 'grp')), may hold values from -6 to 6
- pair_labels: int32 [98304], P('blk'), may hold values from 0 to 98303, as said below
- logit_scale: float32 [1], replicated, may hold values from 1 to 4
- logit_bias: float32 [1], replicated, may hold values from -3 to -1
Outputs:
- mean_loss: float32 [], replicated
- grad_image: float32 [98304, 1152], P(('blk', 'grp'))
- grad_text: float32 [98304, 1152], P(('blk', 'grp'))
Inputs may be any that keep to these rules, and one draw needn't show every extreme that they name: `pair_labels`: the text row that matches an image row lies in a block that is 0 to 3 blocks before the image row's own block, counted around the 384 blocks; several image rows may match one text row.
All inputs are finite; a program needn't handle non-finite values.
Results may differ from a plain program's by a relative error of at most 0.0026.
Values may be sent and summed in bfloat16 or wider, within the bound.
A program may use at most 32 MiB of HBM per device.

v0:
```python
import math

import jax
import jax.numpy as jnp
from jax import lax
from jax.sharding import PartitionSpec as P

STEPS = 4


def from_behind(shard, axis, by):
    size = lax.axis_size(axis)
    return lax.ppermute(shard, axis, [(i, (i + by) % size) for i in range(size)])


def pair_tile(image_rows, row_labels, text_rows, text_ids, factor, shift_bias):
    logits = (
        factor * jnp.dot(image_rows, text_rows.T, preferred_element_type=jnp.float32) + shift_bias
    )
    signs = jnp.where(row_labels[:, None] == text_ids[None, :], 1.0, -1.0).astype(jnp.float32)
    weights = (-signs * jax.nn.sigmoid(-signs * logits)).astype(jnp.bfloat16)
    return (weights, -jnp.sum(jax.nn.log_sigmoid(signs * logits)))


def body(image_embed, text_embed, pair_labels, logit_scale, logit_bias):
    row_count = image_embed.shape[0]
    width = image_embed.shape[1]
    block_count = lax.axis_size("blk")
    group_count = lax.axis_size("grp")
    block_index = lax.axis_index("blk")
    member = lax.axis_index("grp")
    block_rows = row_count * group_count
    factor = logit_scale[0] / math.sqrt(width)
    shift_bias = logit_bias[0]
    row_labels = lax.dynamic_slice_in_dim(pair_labels, member * row_count, row_count)
    text_rows = lax.all_gather(text_embed, "grp", axis=0, tiled=True)
    text_count = text_rows.shape[0]
    positions = jnp.arange(text_count, dtype=jnp.int32)
    image_grad = jnp.zeros(image_embed.shape, jnp.float32)
    text_grad = jnp.zeros(text_rows.shape, jnp.float32)
    loss_part = jnp.zeros((), jnp.float32)
    for loop_step in range(STEPS):
        if loop_step > 0:
            text_rows = from_behind(text_rows, "blk", 1)
            text_grad = from_behind(text_grad, "blk", 1)
        source = (block_index - loop_step) % block_count
        text_ids = source * block_rows + positions
        weights, part = pair_tile(image_embed, row_labels, text_rows, text_ids, factor, shift_bias)
        image_grad = image_grad + factor * jnp.dot(
            weights, text_rows, preferred_element_type=jnp.float32
        )
        loss_part = loss_part + part
        text_grad = text_grad + factor * jnp.dot(
            weights.T, image_embed, preferred_element_type=jnp.float32
        )
    text_grad = from_behind(text_grad, "blk", -(STEPS - 1))
    grad_text = lax.psum_scatter(text_grad, "grp", scatter_dimension=0, tiled=True)
    loss_total = lax.psum(loss_part, ("blk", "grp"))
    mean_loss = loss_total / (block_count * block_rows)
    return (mean_loss, image_grad, grad_text)


def solution(mesh):
    in_specs = (P(("blk", "grp"), None), P(("blk", "grp"), None), P("blk"), P(), P())
    out_specs = (P(), P(("blk", "grp"), None), P(("blk", "grp"), None))
    return jax.shard_map(body, mesh=mesh, in_specs=in_specs, out_specs=out_specs, check_vma=False)
```

profile of v0, /device:TPU:1, one launch (start us, length us, event | category | flops | bytes accessed | tf_op | source)
XLA Modules:
  0.0 300.8 jit_solution(5376779271185490353)
XLA Ops:
  7.2 11.5 %all_gather.3 = bf16[256,1152]{1,0:T(8,128)(2,1)S(1)} all-gather(bf16[128,1152]{1,0:T(8,128)(2,1)} %param.6), channel_id=1, replica_groups=mesh['blk'=384,'grp'=2] {'grp'}, dimensions={0}, use_global_device_ids=true | all-gather | bytes 884736 | tf_op jit(solution)/shard_map/all_gather | solution.py:36
  20.1 0.8 dynamic_slice.3
  20.8 0.3 fusion.5
  21.2 0.5 convolution_multiply_fusion.3
  21.6 8.6 %collective-permute-start.3 = (f32[256,1152]{1,0:T(8,128)S(1)}, f32[256,1152]{1,0:T(8,128)}, u32[]{:S(2)}, u32[]{:S(2)}) collective-permute-start(f32[256,1152]{1,0:T(8,128)S(1)} %convolution_multiply_fusion.3), channel_id=1, source_target_pairs={{0,2},{2,4},{4,6},{6,8},{8,10},{10,12},{12,14},{14,16},{16,18},{18... | collective-permute-start | bytes 3538952 | tf_op jit(solution)/shard_map/ppermute | solution.py:13
  30.2 1.9 collective-permute-start
  32.2 17.5 %collective-permute-done = bf16[256,1152]{1,0:T(8,128)(2,1)S(1)} collective-permute-done((bf16[256,1152]{1,0:T(8,128)(2,1)S(1)}, bf16[256,1152]{1,0:T(8,128)(2,1)S(1)}, u32[]{:S(2)}, u32[]{:S(2)}) %collective-permute-start) | collective-permute-done | bytes 589856 | tf_op jit(solution)/shard_map/ppermute | solution.py:13
  50.0 1.7 fusion
  51.7 4.4 %collective-permute-start.4 = (f32[256,1152]{1,0:T(8,128)S(1)}, f32[256,1152]{1,0:T(8,128)}, u32[]{:S(2)}, u32[]{:S(2)}) collective-permute-start(f32[256,1152]{1,0:T(8,128)S(1)} %fusion), channel_id=1, source_target_pairs={{0,2},{2,4},{4,6},{6,8},{8,10},{10,12},{12,14},{14,16},{16,18},{18... | collective-permute-start | bytes 3538952 | tf_op jit(solution)/shard_map/ppermute | solution.py:13
  56.1 1.9 collective-permute-start.1
  58.1 17.5 %collective-permute-done.1 = bf16[256,1152]{1,0:T(8,128)(2,1)S(1)} collective-permute-done((bf16[256,1152]{1,0:T(8,128)(2,1)S(1)}, bf16[256,1152]{1,0:T(8,128)(2,1)S(1)}, u32[]{:S(2)}, u32[]{:S(2)}) %collective-permute-start.1) | collective-permute-done | bytes 589856 | tf_op jit(solution)/shard_map/ppermute | solution.py:13
  75.9 0.4 convolution_multiply_fusion.1
  76.6 1.4 add.167
  78.0 4.4 %collective-permute-start.5 = (f32[256,1152]{1,0:T(8,128)S(1)}, f32[256,1152]{1,0:T(8,128)}, u32[]{:S(2)}, u32[]{:S(2)}) collective-permute-start(f32[256,1152]{1,0:T(8,128)S(1)} %add.167), channel_id=1, source_target_pairs={{0,2},{2,4},{4,6},{6,8},{8,10},{10,12},{12,14},{14,16},{16,18},{18... | collective-permute-start | bytes 3538952 | tf_op jit(solution)/shard_map/ppermute | solution.py:13
  82.4 1.9 collective-permute-start.2
  84.3 23.1 %collective-permute-done.2 = bf16[256,1152]{1,0:T(8,128)(2,1)} collective-permute-done((bf16[256,1152]{1,0:T(8,128)(2,1)S(1)}, bf16[256,1152]{1,0:T(8,128)(2,1)}, u32[]{:S(2)}, u32[]{:S(2)}) %collective-permute-start.2) | collective-permute-done | bytes 589856 | tf_op jit(solution)/shard_map/ppermute | solution.py:13
  107.4 2.4 fusion.37
  109.8 0.4 convolution_multiply_fusion
  110.5 1.4 add.168
  111.9 18.1 %collective-permute-start.6 = (f32[256,1152]{1,0:T(8,128)S(1)}, f32[256,1152]{1,0:T(8,128)S(1)}, u32[]{:S(2)}, u32[]{:S(2)}) collective-permute-start(f32[256,1152]{1,0:T(8,128)S(1)} %add.168), channel_id=1, source_target_pairs={{0,762},{2,764},{4,766},{6,0},{8,2},{10,4},{12,6},{14,8},{16,10},{... | collective-permute-start | bytes 3538952 | tf_op jit(solution)/shard_map/ppermute | solution.py:13
  130.0 13.8 %collective-permute-done.6 = f32[256,1152]{1,0:T(8,128)S(1)} collective-permute-done((f32[256,1152]{1,0:T(8,128)S(1)}, f32[256,1152]{1,0:T(8,128)S(1)}, u32[]{:S(2)}, u32[]{:S(2)}) %collective-permute-start.6) | collective-permute-done | bytes 1179680 | tf_op jit(solution)/shard_map/ppermute | solution.py:13
  143.8 1.0 copy-done.1
  148.2 141.8 %psum.7 = f32[]{:T(128)} all-reduce(f32[]{:T(128)S(6)} %add.158), channel_id=1, replica_groups=mesh['blk'=384,'grp'=2] {'blk','grp'}, use_global_device_ids=true, to_apply=%region_4.5 | all-reduce | flops 1 | bytes 8 | tf_op jit(solution)/shard_map/psum | solution.py:58
  290.7 2.2 fusion.1
  (26 shorter events, 2.1 us)
Async XLA Ops:
  7.2 13.7 %copy-start = (bf16[128,1152]{1,0:T(8,128)(2,1)S(1)}, bf16[128,1152]{1,0:T(8,128)(2,1)}, u32[]{:S(2)}) copy-start(bf16[128,1152]{1,0:T(8,128)(2,1)} %param.5) | copy-start | bytes 884740
  7.2 285.7 %reduce-scatter.2.cloned.1.call-start = ((), (), s32[]{:S(2)}) async-start(), calls=%async_computation.1 | async-start | bytes 1769472 | tf_op jit(solution)/shard_map/reduce_scatter | solution.py:57
  21.6 28.4 %collective-permute-start.3 = (f32[256,1152]{1,0:T(8,128)S(1)}, f32[256,1152]{1,0:T(8,128)}, u32[]{:S(2)}, u32[]{:S(2)}) collective-permute-start(f32[256,1152]{1,0:T(8,128)S(1)} %convolution_multiply_fusion.3), channel_id=1, source_target_pairs={{0,2},{2,4},{4,6},{6,8},{8,10},{10,12},{12,14},{14,16},{16,18},{18... | collective-permute-start | bytes 3538952 | tf_op jit(solution)/shard_map/ppermute | solution.py:13
  30.2 19.4 %collective-permute-start = (bf16[256,1152]{1,0:T(8,128)(2,1)S(1)}, bf16[256,1152]{1,0:T(8,128)(2,1)S(1)}, u32[]{:S(2)}, u32[]{:S(2)}) collective-permute-start(bf16[256,1152]{1,0:T(8,128)(2,1)S(1)} %all_gather.3), channel_id=1, source_target_pairs={{0,2},{2,4},{4,6},{6,8},{8,10},{10,12},{12,14},{14,16},{16,18},{18... | collective-permute-start | bytes 1769480 | tf_op jit(solution)/shard_map/ppermute | solution.py:13
  51.7 24.8 %collective-permute-start.4 = (f32[256,1152]{1,0:T(8,128)S(1)}, f32[256,1152]{1,0:T(8,128)}, u32[]{:S(2)}, u32[]{:S(2)}) collective-permute-start(f32[256,1152]{1,0:T(8,128)S(1)} %fusion), channel_id=1, source_target_pairs={{0,2},{2,4},{4,6},{6,8},{8,10},{10,12},{12,14},{14,16},{16,18},{18... | collective-permute-start | bytes 3538952 | tf_op jit(solution)/shard_map/ppermute | solution.py:13
  56.1 19.4 %collective-permute-start.1 = (bf16[256,1152]{1,0:T(8,128)(2,1)S(1)}, bf16[256,1152]{1,0:T(8,128)(2,1)S(1)}, u32[]{:S(2)}, u32[]{:S(2)}) collective-permute-start(bf16[256,1152]{1,0:T(8,128)(2,1)S(1)} %collective-permute-done), channel_id=1, source_target_pairs={{0,2},{2,4},{4,6},{6,8},{8,10},{10,12},{12,14},{14,16},{16,18},{18... | collective-permute-start | bytes 1769480 | tf_op jit(solution)/shard_map/ppermute | solution.py:13
  75.9 0.7 copy-start.2
  78.0 32.5 %collective-permute-start.5 = (f32[256,1152]{1,0:T(8,128)S(1)}, f32[256,1152]{1,0:T(8,128)}, u32[]{:S(2)}, u32[]{:S(2)}) collective-permute-start(f32[256,1152]{1,0:T(8,128)S(1)} %add.167), channel_id=1, source_target_pairs={{0,2},{2,4},{4,6},{6,8},{8,10},{10,12},{12,14},{14,16},{16,18},{18... | collective-permute-start | bytes 3538952 | tf_op jit(solution)/shard_map/ppermute | solution.py:13
  82.4 25.0 %collective-permute-start.2 = (bf16[256,1152]{1,0:T(8,128)(2,1)S(1)}, bf16[256,1152]{1,0:T(8,128)(2,1)}, u32[]{:S(2)}, u32[]{:S(2)}) collective-permute-start(bf16[256,1152]{1,0:T(8,128)(2,1)S(1)} %collective-permute-done.1), channel_id=1, source_target_pairs={{0,2},{2,4},{4,6},{6,8},{8,10},{10,12},{12,14},{14,16},{16,18},{18... | collective-permute-start | bytes 1769480 | tf_op jit(solution)/shard_map/ppermute | solution.py:13
  109.8 0.7 copy-start.4
  111.9 31.9 %collective-permute-start.6 = (f32[256,1152]{1,0:T(8,128)S(1)}, f32[256,1152]{1,0:T(8,128)S(1)}, u32[]{:S(2)}, u32[]{:S(2)}) collective-permute-start(f32[256,1152]{1,0:T(8,128)S(1)} %add.168), channel_id=1, source_target_pairs={{0,762},{2,764},{4,766},{6,0},{8,2},{10,4},{12,6},{14,8},{16,10},{... | collective-permute-start | bytes 3538952 | tf_op jit(solution)/shard_map/ppermute | solution.py:13
  143.8 1.0 copy-start.1
  145.1 2.8 copy-start.3
  145.4 145.2 %copy-start.5 = (f32[128,256]{1,0:T(8,128)S(1)}, f32[128,256]{1,0:T(8,128)}, u32[]{:S(2)}) copy-start(f32[128,256]{1,0:T(8,128)} %copy-done.4) | copy-start | bytes 393220
Sparse Core Ops, SparseCore 0:
  144.9 56.4 reduce-scatter.1
where the time goes:
time: 301 us
  blocking collectives  153 us (51%)
  waiting for transfers between devices  71.9 us (24%)
  starting transfers between devices  41.3 us (14%)
  between operations  19.9 us (7%)
  matrix products  9.54 us (3%)
    psum x1, blocking collectives, body(): loss_total = lax.psum(loss_part, ('blk', 'grp'))  142 us
    ppermute x7, waiting for transfers between devices, from_behind(): lax.ppermute(shard, axis, [(i, (i + by) % size) for i in range(size)])  71.8 us
    ppermute x7, starting transfers between devices, from_behind(): lax.ppermute(shard, axis, [(i, (i + by) % size) for i in range(size)])  41.2 us
    all_gather x1, blocking collectives, body(): text_rows = lax.all_gather(text_embed, 'grp', axis=0, tiled=True)  11.5 us
  transfers between devices with their start and end apart: 8, of which 4 were waited for; matrix products, arithmetic and copies ran while one was open for 2% of the time, Pallas kernels for 0%

commit v1 on v0

v1 whole, which is shorter than its diff:
```python
import math

import jax
import jax.numpy as jnp
from jax import lax
from jax.experimental import pallas as pl
from jax.experimental.pallas import tpu as pltpu
from jax.sharding import PartitionSpec as P

STEPS = 4
NT = (((1,), (1,)), ((), ()))
TN = (((0,), (0,)), ((), ()))


def rem_copy(src, dst, send, recv, dev):
    return pltpu.make_async_remote_copy(
        src_ref=src, dst_ref=dst, send_sem=send, recv_sem=recv, device_id=dev,
        device_id_type=pl.DeviceIdType.MESH)


def kernel(image_hbm, text_hbm, labels_hbm, scale_ref, bias_ref,
           loss_ref, grad_image_ref, grad_text_ref,
           images, texts, labels, weights, out_other, in_other, mate_out, mate_in, ext_out, ext_in,
           sum_out, sum_in, loss_xc, loss_y, loss_z, loss_q,
           send, recv, local, xc_send, xc_recv, y_send, y_recv, z_send, z_recv, q_send, q_recv, token):
    rows, width = image_hbm.shape
    blocks = lax.axis_size("blk")
    b = lax.axis_index("blk")
    g = lax.axis_index("grp")
    core = b % 2
    x = (b // 2) % 4
    y = g * 4 + (b // 8) % 4
    z = b // 32
    zq = z // 4
    zr = z % 4

    def at(k):
        return (lax.rem(b + k + blocks, blocks), g)

    def place(x, y, z, core):
        return (((z * 4 + y % 4) * 4 + x) * 2 + core, y // 4)

    partner = (b, 1 - g)
    mate = (b + 1 - 2 * core, g)
    xc_me = x * 2 + core
    xc_peers = [lax.rem(xc_me + i, 8) for i in range(1, 8)]
    y_peers = [lax.rem(y + i, 8) for i in range(1, 8)]
    r_peers = [lax.rem(zr + i, 4) for i in range(1, 4)]
    q_peers = [lax.rem(zq + i, 3) for i in range(1, 3)]
    xc_devs = [place(p // 2, y, z, p % 2) for p in xc_peers]
    y_devs = [place(x, p, z, core) for p in y_peers]
    r_devs = [place(x, y, zq * 4 + p, core) for p in r_peers]
    q_devs = [place(x, y, p * 4 + zr, core) for p in q_peers]

    barrier = pltpu.get_barrier_semaphore()
    greeted = [at(1), at(-1), at(3), at(-3), partner] + xc_devs + y_devs + r_devs
    for dev in greeted:
        pl.semaphore_signal(barrier, inc=1, device_id=dev)

    @pl.when(zq == 1)
    def _():
        for dev in q_devs:
            pl.semaphore_signal(barrier, inc=1, device_id=dev)

    @pl.when(zq != 1)
    def _():
        pl.semaphore_signal(barrier, inc=1, device_id=place(x, y, 4 + zr, core))

    local_copies = [
        pltpu.make_async_copy(image_hbm, images.at[pl.ds(0, rows)], local.at[0]),
        pltpu.make_async_copy(text_hbm, texts.at[0], local.at[1]),
        pltpu.make_async_copy(labels_hbm, labels, local.at[2]),
    ]
    for c in local_copies:
        c.start()

    @pl.when(zq == 1)
    def _():
        pl.semaphore_wait(barrier, len(greeted) + 2)

    @pl.when(zq != 1)
    def _():
        pl.semaphore_wait(barrier, len(greeted) + 1)

    text_1 = rem_copy(text_hbm, texts.at[1], send.at[1], recv.at[1], at(1))
    text_3 = rem_copy(text_hbm, texts.at[3], send.at[3], recv.at[3], at(3))
    image_over = rem_copy(image_hbm, images.at[pl.ds(rows, rows)], send.at[0], recv.at[0], partner)
    text_1.start()
    text_3.start()
    image_over.start()

    @pl.when(zq == 1)
    def _():
        for dev in q_devs:
            pl.semaphore_signal(token, inc=1, device_id=dev)

    factor = scale_ref[0] / math.sqrt(width)
    shift_bias = bias_ref[0]
    for c in local_copies:
        c.wait()
    positions = lax.broadcasted_iota(jnp.int32, (rows, rows), 0) + g * rows

    def tile(slot, half, image_rows):
        logits = factor * lax.dot_general(
            texts[slot], image_rows, NT, preferred_element_type=jnp.float32) + shift_bias
        source = lax.rem(b - slot + blocks, blocks)
        row_labels = labels[pl.ds(g if half == 0 else 1 - g, 1), :]
        match = (positions + source * (2 * rows)) == row_labels
        turned = jnp.where(match, -logits, logits)
        small = jnp.exp(-jnp.abs(turned))
        sig = jnp.where(turned >= 0, 1.0, small) / (1.0 + small)
        weights[slot, :, pl.ds(half * rows, rows)] = jnp.where(match, -sig, sig).astype(jnp.bfloat16)
        terms = jnp.maximum(turned, 0.0) + jnp.log1p(small)
        return jnp.sum(terms.reshape(rows // 8, 8, rows), axis=0)

    own = images[pl.ds(0, rows)]
    total = tile(0, 0, own)
    near, far = 1 + 2 * core, 3 - 2 * core
    rem_copy(text_hbm, texts.at[near], send.at[near], recv.at[near], mate).wait_recv()
    forward = rem_copy(texts.at[near], texts.at[2], send.at[2], recv.at[2], mate)
    forward.start()
    total += tile(near, 0, own)
    rem_copy(text_hbm, texts.at[far], send.at[far], recv.at[far], mate).wait_recv()
    total += tile(far, 0, own)
    forward.wait_recv()
    total += tile(2, 0, own)
    all_texts = texts[...].reshape(STEPS * rows, width)
    acc = lax.dot_general(weights[:, :, pl.ds(0, rows)].reshape(STEPS * rows, rows), all_texts, TN,
                          preferred_element_type=jnp.float32)
    grad_image_ref[...] = acc

    image_over.wait_recv()
    other = images[pl.ds(rows, rows)]
    for slot in range(STEPS):
        total += tile(slot, 1, other)
    out_other[...] = lax.dot_general(
        weights[:, :, pl.ds(rows, rows)].reshape(STEPS * rows, rows), all_texts, TN,
        preferred_element_type=jnp.float32).astype(jnp.bfloat16)
    back = rem_copy(out_other, in_other, send.at[4], recv.at[4], partner)
    back.start()

    loss_xc[xc_me] = total
    xc_copies = [rem_copy(loss_xc.at[xc_me], loss_xc.at[xc_me], xc_send.at[i], xc_recv.at[i], dev)
                 for i, dev in enumerate(xc_devs)]
    for c in xc_copies:
        c.start()

    def partial(slot):
        return jnp.dot(weights[slot], images[...], preferred_element_type=jnp.float32)

    mate_out[...] = partial(2).astype(jnp.bfloat16)
    to_mate = rem_copy(mate_out, mate_in, send.at[5], recv.at[5], mate)
    to_mate.start()
    ext_out[...] = partial(far).astype(jnp.bfloat16)
    to_ext = rem_copy(ext_out, ext_in, send.at[6], recv.at[6], at(2 * core - 3))
    to_ext.start()
    mine = partial(near)
    to_mate.wait_recv()
    sum_out[...] = (mine + mate_in[...].astype(jnp.float32)).astype(jnp.bfloat16)
    to_sum = rem_copy(sum_out, sum_in, send.at[7], recv.at[7], at(-1 - 2 * core))
    to_sum.start()
    grad_text_ref[...] = partial(0)

    def ordered(buffer, count):
        value = buffer[0]
        for i in range(1, count):
            value = value + buffer[i]
        return value

    for c in xc_copies:
        c.wait_recv()
    loss_y[y] = ordered(loss_xc, 8)
    y_copies = [rem_copy(loss_y.at[y], loss_y.at[y], y_send.at[i], y_recv.at[i], dev)
                for i, dev in enumerate(y_devs)]
    for c in y_copies:
        c.start()
    for c in y_copies:
        c.wait_recv()
    loss_z[zr] = ordered(loss_y, 8)
    z_copies = [rem_copy(loss_z.at[zr], loss_z.at[zr], z_send.at[i], z_recv.at[i], dev)
                for i, dev in enumerate(r_devs)]
    for c in z_copies:
        c.start()
    for c in z_copies:
        c.wait_recv()
    loss_q[zq] = ordered(loss_z, 4)

    @pl.when(zq != 1)
    def _():
        pl.semaphore_wait(token, 1)

    q_copies = [rem_copy(loss_q.at[zq], loss_q.at[zq], q_send.at[i], q_recv.at[i], dev)
                for i, dev in enumerate(q_devs)]
    for c in q_copies:
        c.start()

    back.wait_recv()
    grad_image_ref[...] = factor * (grad_image_ref[...] + in_other[...].astype(jnp.float32))
    to_ext.wait_recv()
    to_sum.wait_recv()
    grad_text_ref[...] = factor * (
        grad_text_ref[...] + ext_in[...].astype(jnp.float32) + sum_in[...].astype(jnp.float32))
    for c in q_copies:
        c.wait_recv()
    whole = jnp.sum(jnp.sum(ordered(loss_q, 3), axis=1, keepdims=True), axis=0, keepdims=True)
    loss_ref[...] = whole / (blocks * 2 * rows)
    for c in [text_1, text_3, image_over, forward, back, to_mate, to_ext, to_sum] + xc_copies + y_copies + z_copies + q_copies:
        c.wait_send()


def body(image_embed, text_embed, pair_labels, logit_scale, logit_bias):
    rows, width = image_embed.shape
    shard = pltpu.VMEM((rows, width), jnp.bfloat16)
    dma = pltpu.SemaphoreType.DMA
    tiles = lambda n: pltpu.VMEM((n, 8, 128), jnp.float32)
    any_space = pl.BlockSpec(memory_space=pl.ANY)
    smem = pl.BlockSpec(memory_space=pltpu.SMEM)
    vmem = pl.BlockSpec(memory_space=pltpu.VMEM)
    grad = jax.ShapeDtypeStruct((rows, width), jnp.float32)
    mean_loss, grad_image, grad_text = pl.pallas_call(
        kernel,
        out_shape=(jax.ShapeDtypeStruct((1, 1), jnp.float32), grad, grad),
        in_specs=[any_space, any_space, any_space, smem, smem],
        out_specs=(vmem, vmem, vmem),
        scratch_shapes=[
            pltpu.VMEM((2 * rows, width), jnp.bfloat16),
            pltpu.VMEM((STEPS, rows, width), jnp.bfloat16),
            pltpu.VMEM((2, rows), jnp.int32),
            pltpu.VMEM((STEPS, rows, 2 * rows), jnp.bfloat16),
            shard, shard, shard, shard, shard, shard, shard, shard,
            tiles(8), tiles(8), tiles(4), tiles(3),
            dma((8,)), dma((8,)), dma((3,)),
            dma((7,)), dma((7,)), dma((7,)), dma((7,)), dma((3,)), dma((3,)), dma((2,)), dma((2,)),
            pltpu.SemaphoreType.REGULAR,
        ],
        compiler_params=pltpu.CompilerParams(
            collective_id=0, has_side_effects=True, vmem_limit_bytes=40 * 2**20),
        cost_estimate=pl.CostEstimate(
            flops=6 * 2 * rows * STEPS * rows * width, bytes_accessed=8 * rows * width, transcendentals=0),
        name="band",
    )(image_embed, text_embed, pair_labels.reshape(2, rows), logit_scale, logit_bias)
    return mean_loss.reshape(()), grad_image, grad_text


def solution(mesh):
    in_specs = (P(("blk", "grp"), None), P(("blk", "grp"), None), P("blk"), P(), P())
    out_specs = (P(), P(("blk", "grp"), None), P(("blk", "grp"), None))
    return jax.shard_map(body, mesh=mesh, in_specs=in_specs, out_specs=out_specs, check_vma=False)
```

time: 301 us -> 79.4 us (0.26)
  blocking collectives: 153 us -> 0 us
  waiting for transfers between devices: 71.9 us -> 0 us
  Pallas kernels: 0 us -> 71.2 us
  starting transfers between devices: 41.3 us -> 0 us
  between operations: 19.9 us -> 3.68 us
  matrix products: 9.54 us -> 0 us
    psum x1 -> x0, blocking collectives: 142 us -> none  [body(): loss_total = lax.psum(loss_part, ('blk', 'grp'))]
    ppermute x7 -> x0, waiting for transfers between devices: 71.8 us -> none  [from_behind(): lax.ppermute(shard, axis, [(i, (i + by) % size) for i in range(size)])]
    pallas_call x0 -> x1, Pallas kernels: none -> 71.2 us  [body(): pl.pallas_call(kernel, out_shape=(jax.ShapeDtypeStruct((1, 1), jnp.float3...]
    ppermute x7 -> x0, starting transfers between devices: 41.2 us -> none  [from_behind(): lax.ppermute(shard, axis, [(i, (i + by) % size) for i in range(size)])]
    all_gather x1 -> x0, blocking collectives: 11.5 us -> none  [body(): text_rows = lax.all_gather(text_embed, 'grp', axis=0, tiled=True)]
    dot_general x12 -> x0, matrix products: 9.54 us -> none  [the longest x4 3.35 us: pair_tile(): jnp.dot(image_rows, text_rows.T, preferred_element_type=jnp.float32)]
  transfers between devices with their start and end apart: 8 -> 0, of which waited for: 4 -> 0; matrix products, arithmetic and copies ran while one was open for 2% -> 0% of each run, Pallas kernels for 0% -> 0%
where the time goes in v1:
time: 79.4 us; the launch traced here: 79.1 us
  Pallas kernels  71.2 us (90%)
  local copies, waits for them, and re-layouts  4.23 us (5%)
  between operations  3.68 us (5%)
    pallas_call x1, Pallas kernels, body(): pl.pallas_call(kernel, out_shape=(jax.ShapeDtypeStruct((1, 1), jnp.float3...  71.2 us
    unnamed x8, local copies, waits for them, and re-layouts  4.23 us

profile of v1, /device:TPU:1, one launch (start us, length us, event | category | flops | bytes accessed | tf_op | source)
XLA Modules:
  0.0 79.1 jit_solution(9939663440791120892)
XLA Ops:
  1.9 0.0 copy-start.2
  1.9 0.7 copy-done.2
  2.6 0.0 copy-start
  2.6 1.0 %copy-done = bf16[128,1152]{1,0:T(8,128)(2,1)S(1)} copy-done((bf16[128,1152]{1,0:T(8,128)(2,1)S(1)}, bf16[128,1152]{1,0:T(8,128)(2,1)}, u32[]{:S(2)}) %copy-start) | copy-done | bytes 294936
  3.6 0.0 copy-start.1
  3.6 1.0 %copy-done.1 = bf16[128,1152]{1,0:T(8,128)(2,1)S(1)} copy-done((bf16[128,1152]{1,0:T(8,128)(2,1)S(1)}, bf16[128,1152]{1,0:T(8,128)(2,1)}, u32[]{:S(2)}) %copy-start.1) | copy-done | bytes 294936
  4.5 71.2 %band.1 = (f32[1,1]{1,0:T(1,128)}, f32[128,1152]{1,0:T(8,128)S(1)}, f32[128,1152]{1,0:T(8,128)S(1)}) custom-call(bf16[128,1152]{1,0:T(8,128)(2,1)S(1)} %copy-done, bf16[128,1152]{1,0:T(8,128)(2,1)S(1)} %copy-done.1, s32[2,128]{1,0:T(2,128)S(1)} %bitcast.2, f32[1]{0:T(128)S(6)} %copy.11.scale_ref, f32[1]{0:T(128)S(6)} %copy.12.bias_ref), custom_call_target="tpu_custom_call" | custom-call | flops 905969664 | bytes 1179648 | tf_op jit(solution)/shard_map/band/pallas_call | solution.py:220
  76.4 0.8 %copy.14 = f32[128,1152]{1,0:T(8,128)} copy(f32[128,1152]{1,0:T(8,128)S(1)} %get-tuple-element.13) | data formatting | bytes 1179648
  77.2 0.8 %copy.15 = f32[128,1152]{1,0:T(8,128)} copy(f32[128,1152]{1,0:T(8,128)S(1)} %get-tuple-element.14) | data formatting | bytes 1179648
Async XLA Ops:
  1.9 0.7 copy-start.2
  2.6 1.0 %copy-start = (bf16[128,1152]{1,0:T(8,128)(2,1)S(1)}, bf16[128,1152]{1,0:T(8,128)(2,1)}, u32[]{:S(2)}) copy-start(bf16[128,1152]{1,0:T(8,128)(2,1)} %image_hbm.1) | copy-start | bytes 884740
  3.6 1.0 %copy-start.1 = (bf16[128,1152]{1,0:T(8,128)(2,1)S(1)}, bf16[128,1152]{1,0:T(8,128)(2,1)}, u32[]{:S(2)}) copy-start(bf16[128,1152]{1,0:T(8,128)(2,1)} %text_hbm.1) | copy-start | bytes 884740

commit v2 on v1

v2 whole, which is shorter than its diff:
```python
import math

import jax
import jax.numpy as jnp
from jax import lax
from jax.experimental import pallas as pl
from jax.experimental.pallas import tpu as pltpu
from jax.sharding import PartitionSpec as P

STEPS = 4
CHUNKS = 2
NT = (((1,), (1,)), ((), ()))
TN = (((0,), (0,)), ((), ()))


def rem_copy(src, dst, send, recv, dev):
    return pltpu.make_async_remote_copy(
        src_ref=src, dst_ref=dst, send_sem=send, recv_sem=recv, device_id=dev,
        device_id_type=pl.DeviceIdType.MESH)


def kernel(image_hbm, text_hbm, labels_hbm, scale_ref, bias_ref,
           loss_ref, grad_image_ref, grad_text_ref,
           images, texts, labels, weights, weights_other, relay, out_other, in_other, mate_out, mate_in,
           ext_out, ext_in, sum_out, sum_in, loss_xc, loss_y, loss_z, loss_q,
           send, recv, over_send, over_recv, back_send, back_recv, local, xc_send, xc_recv, y_send, y_recv, z_send, z_recv, q_send, q_recv, token):
    rows, width = image_hbm.shape
    blocks = lax.axis_size("blk")
    b = lax.axis_index("blk")
    g = lax.axis_index("grp")
    core = b % 2
    x = (b // 2) % 4
    y = g * 4 + (b // 8) % 4
    z = b // 32
    zq = z // 4
    zr = z % 4

    def at(k):
        return (lax.rem(b + k + blocks, blocks), g)

    def place(x, y, z, core):
        return (((z * 4 + y % 4) * 4 + x) * 2 + core, y // 4)

    partner = (b, 1 - g)
    mate = (b + 1 - 2 * core, g)
    xc_me = x * 2 + core
    xc_peers = [lax.rem(xc_me + i, 8) for i in range(1, 8)]
    y_peers = [lax.rem(y + i, 8) for i in range(1, 8)]
    r_peers = [lax.rem(zr + i, 4) for i in range(1, 4)]
    q_peers = [lax.rem(zq + i, 3) for i in range(1, 3)]
    xc_devs = [place(p // 2, y, z, p % 2) for p in xc_peers]
    y_devs = [place(x, p, z, core) for p in y_peers]
    r_devs = [place(x, y, zq * 4 + p, core) for p in r_peers]
    q_devs = [place(x, y, p * 4 + zr, core) for p in q_peers]

    barrier = pltpu.get_barrier_semaphore()
    greeted = [at(-k) for k in (1, 2, 3, 8)] + [partner] + xc_devs + y_devs + r_devs
    for dev in greeted:
        pl.semaphore_signal(barrier, inc=1, device_id=dev)

    greeters = len(greeted) + jnp.where(zq == 1, 2, 1)
    for k in (1, 2, 3, 8):
        greeters += jnp.where(b >= k, 1, 0)

        @pl.when(b + k < blocks)
        def _():
            pl.semaphore_signal(barrier, inc=1, device_id=at(k))

    @pl.when(zq == 1)
    def _():
        for dev in q_devs:
            pl.semaphore_signal(barrier, inc=1, device_id=dev)

    @pl.when(zq != 1)
    def _():
        pl.semaphore_signal(barrier, inc=1, device_id=place(x, y, 4 + zr, core))

    local_copies = [
        pltpu.make_async_copy(image_hbm, images.at[pl.ds(0, rows)], local.at[0]),
        pltpu.make_async_copy(text_hbm, texts.at[0], local.at[1]),
        pltpu.make_async_copy(labels_hbm, labels, local.at[2]),
    ]
    for c in local_copies:
        c.start()

    pl.semaphore_wait(barrier, greeters)

    first, last = x == 0, x == 3
    text_1 = rem_copy(text_hbm, texts.at[1], send.at[1], recv.at[1], at(1))
    text_3 = rem_copy(text_hbm, texts.at[3], send.at[3], recv.at[3], at(3))
    text_relay = rem_copy(text_hbm, relay, send.at[3], recv.at[8], at(-5))
    text_1.start()
    direct = ((core == 0) & (x != 3)) | ((core == 1) & (x == 2))
    by_relay = (core == 0) & last

    @pl.when(direct)
    def _():
        text_3.start()

    @pl.when(by_relay)
    def _():
        text_relay.start()

    part = rows // CHUNKS
    over = [rem_copy(image_hbm.at[pl.ds(c * part, part)], images.at[pl.ds(rows + c * part, part)],
                     over_send.at[c], over_recv.at[c], partner) for c in range(CHUNKS)]
    relays_text = (core == 1) & first
    relay_text = rem_copy(relay, texts.at[3], send.at[8], recv.at[3], at(8))
    over[0].start()

    @pl.when(relays_text)
    def _():
        text_relay.wait_recv()
        relay_text.start()

    for c in over[1:]:
        c.start()

    @pl.when(zq == 1)
    def _():
        for dev in q_devs:
            pl.semaphore_signal(token, inc=1, device_id=dev)

    factor = scale_ref[0] / math.sqrt(width)
    shift_bias = bias_ref[0]
    for c in local_copies:
        c.wait()
    own_ids = lax.broadcasted_iota(jnp.int32, (rows, rows), 0) + g * rows
    other_ids = lax.broadcasted_iota(jnp.int32, (rows, rows), 1) + g * rows
    own_labels = labels[pl.ds(g, 1), :]
    other_labels = jnp.broadcast_to(labels[pl.ds(1 - g, 1), :], (rows, rows)).T

    def terms(products, match):
        logits = factor * products + shift_bias
        turned = jnp.where(match, -logits, logits)
        small = jnp.exp(-jnp.abs(turned))
        sig = jnp.where(turned >= 0, 1.0, small) / (1.0 + small)
        loss = jnp.maximum(turned, 0.0) + jnp.log1p(small)
        loss = jnp.sum(loss.reshape(loss.shape[0] // 8, 8, rows), axis=0)
        return jnp.where(match, -sig, sig).astype(jnp.bfloat16), loss

    def first_id(slot):
        return lax.rem(b - slot + blocks, blocks) * (2 * rows)

    own = images[pl.ds(0, rows)]

    def own_tile(slot):
        products = lax.dot_general(texts[slot], own, NT, preferred_element_type=jnp.float32)
        weights[slot], loss = terms(products, own_ids + first_id(slot) == own_labels)
        return loss

    total = own_tile(0)
    near, far = 1 + 2 * core, 3 - 2 * core
    rem_copy(text_hbm, texts.at[near], send.at[near], recv.at[near], mate).wait_recv()
    forward = rem_copy(texts.at[near], texts.at[2], send.at[2], recv.at[2], mate)
    forward.start()
    passes_on = (core == 0) & (x != 3)
    pass_on = rem_copy(texts.at[1], texts.at[3], send.at[4], recv.at[3], at(2))

    @pl.when(passes_on)
    def _():
        pass_on.start()

    total += own_tile(near)
    rem_copy(text_hbm, texts.at[far], send.at[far], recv.at[far], mate).wait_recv()
    total += own_tile(far)
    forward.wait_recv()
    total += own_tile(2)
    all_texts = texts[...].reshape(STEPS * rows, width)
    grad_image_ref[...] = lax.dot_general(
        weights[...].reshape(STEPS * rows, rows), all_texts, TN, preferred_element_type=jnp.float32)

    back = [rem_copy(out_other.at[pl.ds(c * part, part)], in_other.at[pl.ds(c * part, part)],
                     back_send.at[c], back_recv.at[c], partner) for c in range(CHUNKS)]
    z_copies = [rem_copy(loss_z.at[zr], loss_z.at[zr], z_send.at[i], z_recv.at[i], dev)
                for i, dev in enumerate(r_devs)]
    for c in range(CHUNKS):
        over[c].wait_recv()
        here = pl.ds(c * part, part)
        products = lax.dot_general(images[pl.ds(rows + c * part, part)], all_texts, NT,
                                   preferred_element_type=jnp.float32)
        for slot in range(STEPS):
            match = (other_ids[:part] + first_id(slot)) == other_labels[c * part:(c + 1) * part]
            there = pl.ds(slot * rows, rows)
            weights_other[here, there], loss = terms(products[:, slot * rows:(slot + 1) * rows], match)
            total += loss
        if c == CHUNKS - 1:
            loss_z[zr] = total
            for copy in z_copies:
                copy.start()
        out_other[here, :] = jnp.dot(
            weights_other[here, :], all_texts, preferred_element_type=jnp.float32).astype(jnp.bfloat16)
        back[c].start()

    def ordered(buffer, count):
        value = buffer[0]
        for i in range(1, count):
            value = value + buffer[i]
        return value

    def partial(slot):
        column = pl.ds(pl.multiple_of(slot * rows, rows), rows)
        return jnp.dot(weights[slot], own, preferred_element_type=jnp.float32) + lax.dot_general(
            weights_other[:, column], images[pl.ds(rows, rows)], TN, preferred_element_type=jnp.float32)

    mate_out[...] = partial(2).astype(jnp.bfloat16)
    to_mate = rem_copy(mate_out, mate_in, send.at[5], recv.at[5], mate)
    to_mate.start()
    ext_out[...] = partial(far).astype(jnp.bfloat16)
    to_ext = rem_copy(ext_out, ext_in, send.at[6], recv.at[6], at(2 * core - 3))
    ext_relay = rem_copy(ext_out, relay, send.at[6], recv.at[9], at(5))
    ext_by_relay = (core == 0) & first

    @pl.when(ext_by_relay)
    def _():
        ext_relay.start()

    @pl.when(jnp.logical_not(ext_by_relay))
    def _():
        to_ext.start()

    mine = partial(near)
    for c in z_copies:
        c.wait_recv()
    loss_q[zq] = ordered(loss_z, 4)

    @pl.when(zq != 1)
    def _():
        pl.semaphore_wait(token, 1)

    q_copies = [rem_copy(loss_q.at[zq], loss_q.at[zq], q_send.at[i], q_recv.at[i], dev)
                for i, dev in enumerate(q_devs)]
    for c in q_copies:
        c.start()

    to_mate.wait_recv()
    sum_out[...] = (mine + mate_in[...].astype(jnp.float32)).astype(jnp.bfloat16)
    to_sum = rem_copy(sum_out, sum_in, send.at[7], recv.at[7], at(-1 - 2 * core))
    sum_relay = rem_copy(sum_out, relay, send.at[7], recv.at[9], at(5))
    sum_by_relay = (core == 1) & first

    @pl.when(sum_by_relay)
    def _():
        sum_relay.start()

    @pl.when(jnp.logical_not(sum_by_relay))
    def _():
        to_sum.start()

    grad_text_ref[...] = partial(0)

    relays_sum = (core == 0) & last
    relays_ext = (core == 1) & (x == 2)
    relay_sum = rem_copy(relay, sum_in, send.at[9], recv.at[7], at(-8))
    relay_ext = rem_copy(relay, ext_in, send.at[9], recv.at[6], at(-8))

    @pl.when(relays_sum)
    def _():
        sum_relay.wait_recv()
        relay_sum.start()

    @pl.when(relays_ext)
    def _():
        ext_relay.wait_recv()
        relay_ext.start()

    for c in q_copies:
        c.wait_recv()
    loss_y[y] = ordered(loss_q, 3)
    y_copies = [rem_copy(loss_y.at[y], loss_y.at[y], y_send.at[i], y_recv.at[i], dev)
                for i, dev in enumerate(y_devs)]
    for c in y_copies:
        c.start()
    for c in back:
        c.wait_recv()
    grad_image_ref[...] = factor * (grad_image_ref[...] + in_other[...].astype(jnp.float32))
    for c in y_copies:
        c.wait_recv()
    loss_xc[xc_me] = ordered(loss_y, 8)
    xc_copies = [rem_copy(loss_xc.at[xc_me], loss_xc.at[xc_me], xc_send.at[i], xc_recv.at[i], dev)
                 for i, dev in enumerate(xc_devs)]
    for c in xc_copies:
        c.start()
    to_ext.wait_recv()
    to_sum.wait_recv()
    grad_text_ref[...] = factor * (
        grad_text_ref[...] + ext_in[...].astype(jnp.float32) + sum_in[...].astype(jnp.float32))
    for c in xc_copies:
        c.wait_recv()
    whole = jnp.sum(jnp.sum(ordered(loss_xc, 8), axis=1, keepdims=True), axis=0, keepdims=True)
    loss_ref[...] = whole / (blocks * 2 * rows)

    for c in [text_1, forward, to_mate, to_ext, to_sum] + over + back + xc_copies + y_copies + z_copies + q_copies:
        c.wait_send()

    @pl.when(direct | by_relay)
    def _():
        text_3.wait_send()

    @pl.when(relays_text)
    def _():
        relay_text.wait_send()

    @pl.when(passes_on)
    def _():
        pass_on.wait_send()

    @pl.when(relays_sum | relays_ext)
    def _():
        relay_sum.wait_send()


def body(image_embed, text_embed, pair_labels, logit_scale, logit_bias):
    rows, width = image_embed.shape
    shard = pltpu.VMEM((rows, width), jnp.bfloat16)
    dma = pltpu.SemaphoreType.DMA
    tiles = lambda n: pltpu.VMEM((n, 8, 128), jnp.float32)
    hbm = pl.BlockSpec(memory_space=pl.ANY)
    smem = pl.BlockSpec(memory_space=pltpu.SMEM)
    vmem = pl.BlockSpec(memory_space=pltpu.VMEM)
    grad = jax.ShapeDtypeStruct((rows, width), jnp.float32)
    in_hbm = lambda a: pltpu.with_memory_space_constraint(a, pltpu.HBM)
    mean_loss, grad_image, grad_text = pl.pallas_call(
        kernel,
        out_shape=(jax.ShapeDtypeStruct((1, 1), jnp.float32), grad, grad),
        in_specs=[hbm] * 3 + [smem] * 2,
        out_specs=(vmem, vmem, vmem),
        scratch_shapes=[
            pltpu.VMEM((2 * rows, width), jnp.bfloat16),
            pltpu.VMEM((STEPS, rows, width), jnp.bfloat16),
            pltpu.VMEM((2, rows), jnp.int32),
            pltpu.VMEM((STEPS, rows, rows), jnp.bfloat16),
            pltpu.VMEM((rows, STEPS * rows), jnp.bfloat16),
            shard, shard, shard, shard, shard, shard, shard, shard, shard,
            tiles(8), tiles(8), tiles(4), tiles(3),
            dma((10,)), dma((10,)), dma((CHUNKS,)), dma((CHUNKS,)), dma((CHUNKS,)), dma((CHUNKS,)), dma((3,)),
            dma((7,)), dma((7,)), dma((7,)), dma((7,)), dma((3,)), dma((3,)), dma((2,)), dma((2,)),
            pltpu.SemaphoreType.REGULAR,
        ],
        compiler_params=pltpu.CompilerParams(
            collective_id=0, has_side_effects=True, vmem_limit_bytes=40 * 2**20),
        cost_estimate=pl.CostEstimate(
            flops=6 * 2 * rows * STEPS * rows * width, bytes_accessed=8 * rows * width, transcendentals=0),
        name="band",
    )(in_hbm(image_embed), in_hbm(text_embed), in_hbm(pair_labels.reshape(2, rows)), logit_scale, logit_bias)
    return mean_loss.reshape(()), grad_image, grad_text


def solution(mesh):
    in_specs = (P(("blk", "grp"), None), P(("blk", "grp"), None), P("blk"), P(), P())
    out_specs = (P(), P(("blk", "grp"), None), P(("blk", "grp"), None))
    return jax.shard_map(body, mesh=mesh, in_specs=in_specs, out_specs=out_specs, check_vma=False)
```

time: 79.4 us -> 72.7 us (0.916)
  Pallas kernels: 71.2 us -> 67.2 us
  local copies, waits for them, and re-layouts: 4.23 us -> 1.63 us
    pallas_call x1, Pallas kernels: 71.2 us -> 67.2 us  [body(): pl.pallas_call(kernel, out_shape=(jax.ShapeDtypeStruct((1, 1), jnp.float3...]
    unnamed x8 -> x2, local copies, waits for them, and re-layouts: 4.23 us -> 1.63 us
where the time goes in v2:
time: 72.7 us; the launch traced here: 72.5 us
  Pallas kernels  67.2 us (92%)
  between operations  3.62 us (5%)
  local copies, waits for them, and re-layouts  1.63 us (2%)
    pallas_call x1, Pallas kernels, body(): pl.pallas_call(kernel, out_shape=(jax.ShapeDtypeStruct((1, 1), jnp.float3...  67.2 us
    unnamed x2, local copies, waits for them, and re-layouts  1.63 us

profile of v2, /device:TPU:1, one launch (start us, length us, event | category | flops | bytes accessed | tf_op | source)
XLA Modules:
  0.0 72.5 jit_solution(3145535364331723801)
XLA Ops:
  1.9 67.2 %band.1 = (f32[1,1]{1,0:T(1,128)}, f32[128,1152]{1,0:T(8,128)S(1)}, f32[128,1152]{1,0:T(8,128)S(1)}) custom-call(bf16[128,1152]{1,0:T(8,128)(2,1)} %image_hbm.1, bf16[128,1152]{1,0:T(8,128)(2,1)} %text_hbm.1, s32[2,128]{1,0:T(2,128)} %bitcast.2, f32[1]{0:T(128)S(6)} %copy.11.scale_ref, f32[1]{0:T(128)S(6)} %copy.12.bias_ref), custom_call_target="tpu_custom_call" | custom-call | flops 905969664 | bytes 1179648 | tf_op jit(solution)/shard_map/band/pallas_call | solution.py:323
  69.7 0.8 %copy.14 = f32[128,1152]{1,0:T(8,128)} copy(f32[128,1152]{1,0:T(8,128)S(1)} %get-tuple-element.13) | data formatting | bytes 1179648
  70.5 0.8 %copy.15 = f32[128,1152]{1,0:T(8,128)} copy(f32[128,1152]{1,0:T(8,128)S(1)} %get-tuple-element.14) | data formatting | bytes 1179648

commit v3 on v2

--- a/solution.py
+++ b/solution.py
@@ -22,8 +22,8 @@
 def kernel(image_hbm, text_hbm, labels_hbm, scale_ref, bias_ref,
            loss_ref, grad_image_ref, grad_text_ref,
            images, texts, labels, weights, weights_other, relay, out_other, in_other, mate_out, mate_in,
-           ext_out, ext_in, sum_out, sum_in, loss_xc, loss_y, loss_z, loss_q,
-           send, recv, over_send, over_recv, back_send, back_recv, local, xc_send, xc_recv, y_send, y_recv, z_send, z_recv, q_send, q_recv, token):
+           ext_out, ext_in, sum_out, sum_in, loss_xc, loss_y, loss_z,
+           send, recv, over_send, over_recv, back_send, back_recv, local, xc_send, xc_recv, y_send, y_recv, z_send, z_recv, token):
     rows, width = image_hbm.shape
     blocks = lax.axis_size("blk")
     b = lax.axis_index("blk")
@@ -51,15 +51,16 @@
     xc_devs = [place(p // 2, y, z, p % 2) for p in xc_peers]
     y_devs = [place(x, p, z, core) for p in y_peers]
     r_devs = [place(x, y, zq * 4 + p, core) for p in r_peers]
+    z_devs = [place(x, y, lax.rem(z + i, 12), core) for i in range(1, 12)]
     q_devs = [place(x, y, p * 4 + zr, core) for p in q_peers]
 
     barrier = pltpu.get_barrier_semaphore()
-    greeted = [at(-k) for k in (1, 2, 3, 8)] + [partner] + xc_devs + y_devs + r_devs
+    greeted = [at(-k) for k in (1, 2, 3, 6, 8)] + [partner] + xc_devs + y_devs + r_devs
     for dev in greeted:
         pl.semaphore_signal(barrier, inc=1, device_id=dev)
 
     greeters = len(greeted) + jnp.where(zq == 1, 2, 1)
-    for k in (1, 2, 3, 8):
+    for k in (1, 2, 3, 6, 8):
         greeters += jnp.where(b >= k, 1, 0)
 
         @pl.when(b + k < blocks)
@@ -88,7 +89,7 @@
     first, last = x == 0, x == 3
     text_1 = rem_copy(text_hbm, texts.at[1], send.at[1], recv.at[1], at(1))
     text_3 = rem_copy(text_hbm, texts.at[3], send.at[3], recv.at[3], at(3))
-    text_relay = rem_copy(text_hbm, relay, send.at[3], recv.at[8], at(-5))
+    text_relay = rem_copy(text_hbm, relay, send.at[3], recv.at[8], at(-3))
     text_1.start()
     direct = ((core == 0) & (x != 3)) | ((core == 1) & (x == 2))
     by_relay = (core == 0) & last
@@ -104,8 +105,8 @@
     part = rows // CHUNKS
     over = [rem_copy(image_hbm.at[pl.ds(c * part, part)], images.at[pl.ds(rows + c * part, part)],
                      over_send.at[c], over_recv.at[c], partner) for c in range(CHUNKS)]
-    relays_text = (core == 1) & first
-    relay_text = rem_copy(relay, texts.at[3], send.at[8], recv.at[3], at(8))
+    relays_text = (core == 1) & (x == 1)
+    relay_text = rem_copy(relay, texts.at[3], send.at[8], recv.at[3], at(6))
     over[0].start()
 
     @pl.when(relays_text)
@@ -119,7 +120,7 @@
     @pl.when(zq == 1)
     def _():
         for dev in q_devs:
-            pl.semaphore_signal(token, inc=1, device_id=dev)
+            pl.semaphore_signal(token.at[0], inc=1, device_id=dev)
 
     factor = scale_ref[0] / math.sqrt(width)
     shift_bias = bias_ref[0]
@@ -161,6 +162,12 @@
     def _():
         pass_on.start()
 
+    @pl.when(zq != 1)
+    def _():
+        pl.semaphore_wait(token.at[0], 1)
+        for dev in q_devs:
+            pl.semaphore_signal(token.at[1], inc=1, device_id=dev)
+
     total += own_tile(near)
     rem_copy(text_hbm, texts.at[far], send.at[far], recv.at[far], mate).wait_recv()
     total += own_tile(far)
@@ -172,8 +179,8 @@
 
     back = [rem_copy(out_other.at[pl.ds(c * part, part)], in_other.at[pl.ds(c * part, part)],
                      back_send.at[c], back_recv.at[c], partner) for c in range(CHUNKS)]
-    z_copies = [rem_copy(loss_z.at[zr], loss_z.at[zr], z_send.at[i], z_recv.at[i], dev)
-                for i, dev in enumerate(r_devs)]
+    z_copies = [rem_copy(loss_z.at[z], loss_z.at[z], z_send.at[i], z_recv.at[i], dev)
+                for i, dev in enumerate(z_devs)]
     for c in range(CHUNKS):
         over[c].wait_recv()
         here = pl.ds(c * part, part)
@@ -185,7 +192,8 @@
             weights_other[here, there], loss = terms(products[:, slot * rows:(slot + 1) * rows], match)
             total += loss
         if c == CHUNKS - 1:
-            loss_z[zr] = total
+            loss_z[z] = total
+            pl.semaphore_wait(token.at[1], jnp.where(zq == 1, 2, 1))
             for copy in z_copies:
                 copy.start()
         out_other[here, :] = jnp.dot(
@@ -220,19 +228,6 @@
         to_ext.start()
 
     mine = partial(near)
-    for c in z_copies:
-        c.wait_recv()
-    loss_q[zq] = ordered(loss_z, 4)
-
-    @pl.when(zq != 1)
-    def _():
-        pl.semaphore_wait(token, 1)
-
-    q_copies = [rem_copy(loss_q.at[zq], loss_q.at[zq], q_send.at[i], q_recv.at[i], dev)
-                for i, dev in enumerate(q_devs)]
-    for c in q_copies:
-        c.start()
-
     to_mate.wait_recv()
     sum_out[...] = (mine + mate_in[...].astype(jnp.float32)).astype(jnp.bfloat16)
     to_sum = rem_copy(sum_out, sum_in, send.at[7], recv.at[7], at(-1 - 2 * core))
@@ -264,9 +259,9 @@
         ext_relay.wait_recv()
         relay_ext.start()
 
-    for c in q_copies:
+    for c in z_copies:
         c.wait_recv()
-    loss_y[y] = ordered(loss_q, 3)
+    loss_y[y] = ordered(loss_z, 12)
     y_copies = [rem_copy(loss_y.at[y], loss_y.at[y], y_send.at[i], y_recv.at[i], dev)
                 for i, dev in enumerate(y_devs)]
     for c in y_copies:
@@ -290,7 +285,7 @@
     whole = jnp.sum(jnp.sum(ordered(loss_xc, 8), axis=1, keepdims=True), axis=0, keepdims=True)
     loss_ref[...] = whole / (blocks * 2 * rows)
 
-    for c in [text_1, forward, to_mate, to_ext, to_sum] + over + back + xc_copies + y_copies + z_copies + q_copies:
+    for c in [text_1, forward, to_mate, to_ext, to_sum] + over + back + xc_copies + y_copies + z_copies:
         c.wait_send()
 
     @pl.when(direct | by_relay)
@@ -332,10 +327,10 @@
             pltpu.VMEM((STEPS, rows, rows), jnp.bfloat16),
             pltpu.VMEM((rows, STEPS * rows), jnp.bfloat16),
             shard, shard, shard, shard, shard, shard, shard, shard, shard,
-            tiles(8), tiles(8), tiles(4), tiles(3),
+            tiles(8), tiles(8), tiles(12),
             dma((10,)), dma((10,)), dma((CHUNKS,)), dma((CHUNKS,)), dma((CHUNKS,)), dma((CHUNKS,)), dma((3,)),
-            dma((7,)), dma((7,)), dma((7,)), dma((7,)), dma((3,)), dma((3,)), dma((2,)), dma((2,)),
-            pltpu.SemaphoreType.REGULAR,
+            dma((7,)), dma((7,)), dma((7,)), dma((7,)), dma((11,)), dma((11,)),
+            pltpu.SemaphoreType.REGULAR((2,)),
         ],
         compiler_params=pltpu.CompilerParams(
             collective_id=0, has_side_effects=True, vmem_limit_bytes=40 * 2**20),

time: 72.7 us -> 65.4 us (0.90)
  Pallas kernels: 67.2 us -> 60 us
    pallas_call x1, Pallas kernels: 67.2 us -> 60 us  [body(): pl.pallas_call(kernel, out_shape=(jax.ShapeDtypeStruct((1, 1), jnp.float3...]
where the time goes in v3:
time: 65.4 us; the launch traced here: 65.2 us
  Pallas kernels  60 us (92%)
  between operations  3.62 us (6%)
  local copies, waits for them, and re-layouts  1.63 us (2%)
    pallas_call x1, Pallas kernels, body(): pl.pallas_call(kernel, out_shape=(jax.ShapeDtypeStruct((1, 1), jnp.float3...  60 us
    unnamed x2, local copies, waits for them, and re-layouts  1.63 us

profile of v3, /device:TPU:1, one launch (start us, length us, event | category | flops | bytes accessed | tf_op | source)
XLA Modules:
  0.0 65.2 jit_solution(15615735857470611925)
XLA Ops:
  1.9 60.0 %band.1 = (f32[1,1]{1,0:T(1,128)}, f32[128,1152]{1,0:T(8,128)S(1)}, f32[128,1152]{1,0:T(8,128)S(1)}) custom-call(bf16[128,1152]{1,0:T(8,128)(2,1)} %image_hbm.1, bf16[128,1152]{1,0:T(8,128)(2,1)} %text_hbm.1, s32[2,128]{1,0:T(2,128)} %bitcast.2, f32[1]{0:T(128)S(6)} %copy.11.scale_ref, f32[1]{0:T(128)S(6)} %copy.12.bias_ref), custom_call_target="tpu_custom_call" | custom-call | flops 905969664 | bytes 1179648 | tf_op jit(solution)/shard_map/band/pallas_call | solution.py:318
  62.5 0.8 %copy.14 = f32[128,1152]{1,0:T(8,128)} copy(f32[128,1152]{1,0:T(8,128)S(1)} %get-tuple-element.13) | data formatting | bytes 1179648
  63.3 0.8 %copy.15 = f32[128,1152]{1,0:T(8,128)} copy(f32[128,1152]{1,0:T(8,128)S(1)} %get-tuple-element.14) | data formatting | bytes 1179648

commit v4 on v3

--- a/solution.py
+++ b/solution.py
@@ -8,7 +8,7 @@
 from jax.sharding import PartitionSpec as P
 
 STEPS = 4
-CHUNKS = 2
+CHUNKS = 1
 NT = (((1,), (1,)), ((), ()))
 TN = (((0,), (0,)), ((), ()))
 
@@ -55,17 +55,17 @@
     q_devs = [place(x, y, p * 4 + zr, core) for p in q_peers]
 
     barrier = pltpu.get_barrier_semaphore()
-    greeted = [at(-k) for k in (1, 2, 3, 6, 8)] + [partner] + xc_devs + y_devs + r_devs
+    greeted = [partner] + xc_devs + y_devs + r_devs
     for dev in greeted:
         pl.semaphore_signal(barrier, inc=1, device_id=dev)
 
-    greeters = len(greeted) + jnp.where(zq == 1, 2, 1)
-    for k in (1, 2, 3, 6, 8):
-        greeters += jnp.where(b >= k, 1, 0)
-
-        @pl.when(b + k < blocks)
-        def _():
-            pl.semaphore_signal(barrier, inc=1, device_id=at(k))
+    head = (x == 0) & (core == 1)
+    greeters = len(greeted) + jnp.where(zq == 1, 2, 1) + jnp.where((x > 0) & (core == 1), 1, 0)
+
+    @pl.when(head)
+    def _():
+        for k in (2, 4, 6):
+            pl.semaphore_signal(barrier, inc=1, device_id=at(-k))
 
     @pl.when(zq == 1)
     def _():
@@ -87,12 +87,14 @@
     pl.semaphore_wait(barrier, greeters)
 
     first, last = x == 0, x == 3
-    text_1 = rem_copy(text_hbm, texts.at[1], send.at[1], recv.at[1], at(1))
+    crosses = last & (core == 1)
+    one = jnp.where(crosses, 2, 1)
+    text_1 = rem_copy(text_hbm, texts.at[one], send.at[1], recv.at[one], at(one))
     text_3 = rem_copy(text_hbm, texts.at[3], send.at[3], recv.at[3], at(3))
-    text_relay = rem_copy(text_hbm, relay, send.at[3], recv.at[8], at(-3))
+    text_relay = rem_copy(text_hbm, relay, send.at[3], recv.at[8], at(jnp.where(core == 0, -3, 4)))
     text_1.start()
-    direct = ((core == 0) & (x != 3)) | ((core == 1) & (x == 2))
-    by_relay = (core == 0) & last
+    direct = (core == 0) & (x != 3)
+    by_relay = ((core == 0) & last) | ((core == 1) & (x == 2))
 
     @pl.when(direct)
     def _():
@@ -106,7 +108,7 @@
     over = [rem_copy(image_hbm.at[pl.ds(c * part, part)], images.at[pl.ds(rows + c * part, part)],
                      over_send.at[c], over_recv.at[c], partner) for c in range(CHUNKS)]
     relays_text = (core == 1) & (x == 1)
-    relay_text = rem_copy(relay, texts.at[3], send.at[8], recv.at[3], at(6))
+    relay_text = rem_copy(relay, texts.at[3], send.at[8], recv.at[3], at(jnp.where(x == 1, 6, -1)))
     over[0].start()
 
     @pl.when(relays_text)
@@ -122,10 +124,10 @@
         for dev in q_devs:
             pl.semaphore_signal(token.at[0], inc=1, device_id=dev)
 
+    for c in local_copies:
+        c.wait()
     factor = scale_ref[0] / math.sqrt(width)
     shift_bias = bias_ref[0]
-    for c in local_copies:
-        c.wait()
     own_ids = lax.broadcasted_iota(jnp.int32, (rows, rows), 0) + g * rows
     other_ids = lax.broadcasted_iota(jnp.int32, (rows, rows), 1) + g * rows
     own_labels = labels[pl.ds(g, 1), :]
@@ -152,11 +154,23 @@
 
     total = own_tile(0)
     near, far = 1 + 2 * core, 3 - 2 * core
-    rem_copy(text_hbm, texts.at[near], send.at[near], recv.at[near], mate).wait_recv()
-    forward = rem_copy(texts.at[near], texts.at[2], send.at[2], recv.at[2], mate)
-    forward.start()
-    passes_on = (core == 0) & (x != 3)
-    pass_on = rem_copy(texts.at[1], texts.at[3], send.at[4], recv.at[3], at(2))
+    def arrival(slot):
+        return rem_copy(text_hbm, texts.at[slot], send.at[0], recv.at[slot], mate)
+
+    next_slots = [jnp.where(first, jnp.where(core == 1, 2, 1), near),
+                  jnp.where(first, 3, far),
+                  jnp.where(head, 1, 2)]
+    goes = jnp.where(head, 1, 2)
+    forwards = jnp.logical_not(first & (core == 0))
+    passes_on = ((core == 0) & ((x == 1) | (x == 2))) | head
+    forward = rem_copy(texts.at[next_slots[0]], texts.at[goes], send.at[2], recv.at[goes], mate)
+    pass_on = rem_copy(texts.at[next_slots[0]], texts.at[3], send.at[4], recv.at[3], at(jnp.where(core == 0, 2, 1)))
+    forward_2 = rem_copy(texts.at[3], texts.at[2], send.at[0], recv.at[2], mate)
+    arrival(next_slots[0]).wait_recv()
+
+    @pl.when(forwards)
+    def _():
+        forward.start()
 
     @pl.when(passes_on)
     def _():
@@ -168,11 +182,21 @@
         for dev in q_devs:
             pl.semaphore_signal(token.at[1], inc=1, device_id=dev)
 
-    total += own_tile(near)
-    rem_copy(text_hbm, texts.at[far], send.at[far], recv.at[far], mate).wait_recv()
-    total += own_tile(far)
-    forward.wait_recv()
-    total += own_tile(2)
+    @pl.when(head)
+    def _():
+        text_relay.wait_recv()
+        relay_text.start()
+
+    total += own_tile(next_slots[0])
+    arrival(next_slots[1]).wait_recv()
+
+    @pl.when(head)
+    def _():
+        forward_2.start()
+
+    total += own_tile(next_slots[1])
+    arrival(next_slots[2]).wait_recv()
+    total += own_tile(next_slots[2])
     all_texts = texts[...].reshape(STEPS * rows, width)
     grad_image_ref[...] = lax.dot_general(
         weights[...].reshape(STEPS * rows, rows), all_texts, TN, preferred_element_type=jnp.float32)
@@ -285,16 +309,24 @@
     whole = jnp.sum(jnp.sum(ordered(loss_xc, 8), axis=1, keepdims=True), axis=0, keepdims=True)
     loss_ref[...] = whole / (blocks * 2 * rows)
 
-    for c in [text_1, forward, to_mate, to_ext, to_sum] + over + back + xc_copies + y_copies + z_copies:
+    for c in [text_1, to_mate, to_ext, to_sum] + over + back + xc_copies + y_copies + z_copies:
         c.wait_send()
 
     @pl.when(direct | by_relay)
     def _():
         text_3.wait_send()
 
-    @pl.when(relays_text)
+    @pl.when(relays_text | head)
     def _():
         relay_text.wait_send()
+
+    @pl.when(forwards)
+    def _():
+        forward.wait_send()
+
+    @pl.when(head)
+    def _():
+        forward_2.wait_send()
 
     @pl.when(passes_on)
     def _():
@@ -337,7 +369,8 @@
         cost_estimate=pl.CostEstimate(
             flops=6 * 2 * rows * STEPS * rows * width, bytes_accessed=8 * rows * width, transcendentals=0),
         name="band",
-    )(in_hbm(image_embed), in_hbm(text_embed), in_hbm(pair_labels.reshape(2, rows)), logit_scale, logit_bias)
+    )(in_hbm(image_embed), in_hbm(text_embed), in_hbm(pair_labels.reshape(2, rows)),
+      logit_scale, logit_bias)
     return mean_loss.reshape(()), grad_image, grad_text
 
 

time: 65.4 us -> 64.2 us (0.982)
  Pallas kernels: 60 us -> 58.7 us
    pallas_call x1, Pallas kernels: 60 us -> 58.7 us  [body(): pl.pallas_call(kernel, out_shape=(jax.ShapeDtypeStruct((1, 1), jnp.float3...]
where the time goes in v4:
time: 64.2 us; the launch traced here: 64 us
  Pallas kernels  58.7 us (91%)
  between operations  3.62 us (6%)
  local copies, waits for them, and re-layouts  1.63 us (3%)
    pallas_call x1, Pallas kernels, body(): pl.pallas_call(kernel, out_shape=(jax.ShapeDtypeStruct((1, 1), jnp.float3...  58.7 us
    unnamed x2, local copies, waits for them, and re-layouts  1.63 us

profile of v4, /device:TPU:1, one launch (start us, length us, event | category | flops | bytes accessed | tf_op | source)
XLA Modules:
  0.0 64.0 jit_solution(14919210084298051016)
XLA Ops:
  1.9 58.7 %band.1 = (f32[1,1]{1,0:T(1,128)}, f32[128,1152]{1,0:T(8,128)S(1)}, f32[128,1152]{1,0:T(8,128)S(1)}) custom-call(bf16[128,1152]{1,0:T(8,128)(2,1)} %image_hbm.1, bf16[128,1152]{1,0:T(8,128)(2,1)} %text_hbm.1, s32[2,128]{1,0:T(2,128)} %bitcast.2, f32[1]{0:T(128)S(6)} %copy.11.scale_ref, f32[1]{0:T(128)S(6)} %copy.12.bias_ref), custom_call_target="tpu_custom_call" | custom-call | flops 905969664 | bytes 1179648 | tf_op jit(solution)/shard_map/band/pallas_call | solution.py:350
  61.2 0.8 %copy.14 = f32[128,1152]{1,0:T(8,128)} copy(f32[128,1152]{1,0:T(8,128)S(1)} %get-tuple-element.13) | data formatting | bytes 1179648
  62.0 0.8 %copy.15 = f32[128,1152]{1,0:T(8,128)} copy(f32[128,1152]{1,0:T(8,128)S(1)} %get-tuple-element.14) | data formatting | bytes 1179648

commit v5 on v4

--- a/solution.py
+++ b/solution.py
@@ -8,7 +8,7 @@
 from jax.sharding import PartitionSpec as P
 
 STEPS = 4
-CHUNKS = 1
+CHUNKS = 2
 NT = (((1,), (1,)), ((), ()))
 TN = (((0,), (0,)), ((), ()))
 
@@ -222,7 +222,9 @@
                 copy.start()
         out_other[here, :] = jnp.dot(
             weights_other[here, :], all_texts, preferred_element_type=jnp.float32).astype(jnp.bfloat16)
-        back[c].start()
+
+    for c in back:
+        c.start()
 
     def ordered(buffer, count):
         value = buffer[0]
@@ -268,21 +270,6 @@
 
     grad_text_ref[...] = partial(0)
 
-    relays_sum = (core == 0) & last
-    relays_ext = (core == 1) & (x == 2)
-    relay_sum = rem_copy(relay, sum_in, send.at[9], recv.at[7], at(-8))
-    relay_ext = rem_copy(relay, ext_in, send.at[9], recv.at[6], at(-8))
-
-    @pl.when(relays_sum)
-    def _():
-        sum_relay.wait_recv()
-        relay_sum.start()
-
-    @pl.when(relays_ext)
-    def _():
-        ext_relay.wait_recv()
-        relay_ext.start()
-
     for c in z_copies:
         c.wait_recv()
     loss_y[y] = ordered(loss_z, 12)
@@ -290,6 +277,22 @@
                 for i, dev in enumerate(y_devs)]
     for c in y_copies:
         c.start()
+
+    relays_sum = (core == 0) & last
+    relays_ext = (core == 1) & (x == 2)
+    relay_sum = rem_copy(relay, sum_in, send.at[9], recv.at[7], at(-8))
+    relay_ext = rem_copy(relay, ext_in, send.at[9], recv.at[6], at(-8))
+
+    @pl.when(relays_sum)
+    def _():
+        sum_relay.wait_recv()
+        relay_sum.start()
+
+    @pl.when(relays_ext)
+    def _():
+        ext_relay.wait_recv()
+        relay_ext.start()
+
     for c in back:
         c.wait_recv()
     grad_image_ref[...] = factor * (grad_image_ref[...] + in_other[...].astype(jnp.float32))
@@ -335,6 +338,15 @@
     @pl.when(relays_sum | relays_ext)
     def _():
         relay_sum.wait_send()
+
+
+def hand_over(loss_in, image_in, text_in, loss_out, image_out, text_out, sems):
+    copies = [pltpu.make_async_copy(a, o, sems.at[i]) for i, (a, o) in enumerate(
+        [(image_in, image_out), (text_in, text_out), (loss_in, loss_out)])]
+    for c in copies:
+        c.start()
+    for c in copies:
+        c.wait()
 
 
 def body(image_embed, text_embed, pair_labels, logit_scale, logit_bias):
@@ -371,6 +383,15 @@
         name="band",
     )(in_hbm(image_embed), in_hbm(text_embed), in_hbm(pair_labels.reshape(2, rows)),
       logit_scale, logit_bias)
+    in_vmem = lambda a: pltpu.with_memory_space_constraint(a, pltpu.VMEM)
+    mean_loss, grad_image, grad_text = pl.pallas_call(
+        hand_over,
+        out_shape=(jax.ShapeDtypeStruct((1, 1), jnp.float32), grad, grad),
+        in_specs=[hbm] * 3,
+        out_specs=(hbm, hbm, hbm),
+        scratch_shapes=[dma((3,))],
+        name="hand_over",
+    )(in_vmem(mean_loss), in_vmem(grad_image), in_vmem(grad_text))
     return mean_loss.reshape(()), grad_image, grad_text
 
 

time: 64.2 us -> 62.1 us (0.967)
  between operations: 3.62 us -> 1.93 us
  local copies, waits for them, and re-layouts: 1.63 us -> 0 us
  Pallas kernels: 58.7 us -> 60 us
    pallas_call x0 -> x1, Pallas kernels: none -> 1.67 us  [body(): pl.pallas_call(hand_over, out_shape=(jax.ShapeDtypeStruct((1, 1), jnp.flo...]
    unnamed x2 -> x0, local copies, waits for them, and re-layouts: 1.63 us -> none
where the time goes in v5:
time: 62.1 us; the launch traced here: 61.9 us
  Pallas kernels  60 us (97%)
  between operations  1.93 us (3%)
    pallas_call x1, Pallas kernels, body(): pl.pallas_call(kernel, out_shape=(jax.ShapeDtypeStruct((1, 1), jnp.float3...  58.3 us
    pallas_call x1, Pallas kernels, body(): pl.pallas_call(hand_over, out_shape=(jax.ShapeDtypeStruct((1, 1), jnp.flo...  1.67 us

profile of v5, /device:TPU:1, one launch (start us, length us, event | category | flops | bytes accessed | tf_op | source)
XLA Modules:
  0.0 61.9 jit_solution(3500537227038964945)
XLA Ops:
  1.9 58.3 %band.1 = (f32[1,1]{1,0:T(1,128)}, f32[128,1152]{1,0:T(8,128)S(1)}, f32[128,1152]{1,0:T(8,128)S(1)}) custom-call(bf16[128,1152]{1,0:T(8,128)(2,1)} %image_hbm.1, bf16[128,1152]{1,0:T(8,128)(2,1)} %text_hbm.1, s32[2,128]{1,0:T(2,128)} %bitcast.2, f32[1]{0:T(128)S(6)} %copy.8.scale_ref, f32[1]{0:T(128)S(6)} %copy.9.bias_ref), custom_call_target="tpu_custom_call" | custom-call | flops 905969664 | bytes 1179648 | tf_op jit(solution)/shard_map/band/pallas_call | solution.py:362
  60.2 1.7 %hand_over.1 = (f32[1,1]{1,0:T(1,128)}, f32[128,1152]{1,0:T(8,128)}, f32[128,1152]{1,0:T(8,128)}) custom-call(f32[1,1]{1,0:T(1,128)} %get-tuple-element.9.loss_in, f32[128,1152]{1,0:T(8,128)S(1)} %get-tuple-element.10.image_in, f32[128,1152]{1,0:T(8,128)S(1)} %get-tuple-element.11.text_in), custom_call_target="tpu_custom_call" | custom-call | tf_op jit(solution)/shard_map/hand_over/pallas_call | solution.py:387

commit v6 on v5

--- a/solution.py
+++ b/solution.py
@@ -203,8 +203,8 @@
 
     back = [rem_copy(out_other.at[pl.ds(c * part, part)], in_other.at[pl.ds(c * part, part)],
                      back_send.at[c], back_recv.at[c], partner) for c in range(CHUNKS)]
-    z_copies = [rem_copy(loss_z.at[z], loss_z.at[z], z_send.at[i], z_recv.at[i], dev)
-                for i, dev in enumerate(z_devs)]
+    xc_copies = [rem_copy(loss_xc.at[xc_me], loss_xc.at[xc_me], xc_send.at[i], xc_recv.at[i], dev)
+                 for i, dev in enumerate(xc_devs)]
     for c in range(CHUNKS):
         over[c].wait_recv()
         here = pl.ds(c * part, part)
@@ -216,9 +216,8 @@
             weights_other[here, there], loss = terms(products[:, slot * rows:(slot + 1) * rows], match)
             total += loss
         if c == CHUNKS - 1:
-            loss_z[z] = total
-            pl.semaphore_wait(token.at[1], jnp.where(zq == 1, 2, 1))
-            for copy in z_copies:
+            loss_xc[xc_me] = total
+            for copy in xc_copies:
                 copy.start()
         out_other[here, :] = jnp.dot(
             weights_other[here, :], all_texts, preferred_element_type=jnp.float32).astype(jnp.bfloat16)
@@ -268,6 +267,15 @@
     def _():
         to_sum.start()
 
+    for c in xc_copies:
+        c.wait_recv()
+    loss_z[z] = ordered(loss_xc, 8)
+    pl.semaphore_wait(token.at[1], jnp.where(zq == 1, 2, 1))
+    z_copies = [rem_copy(loss_z.at[z], loss_z.at[z], z_send.at[i], z_recv.at[i], dev)
+                for i, dev in enumerate(z_devs)]
+    for c in z_copies:
+        c.start()
+
     grad_text_ref[...] = partial(0)
 
     for c in z_copies:
@@ -296,20 +304,13 @@
     for c in back:
         c.wait_recv()
     grad_image_ref[...] = factor * (grad_image_ref[...] + in_other[...].astype(jnp.float32))
-    for c in y_copies:
-        c.wait_recv()
-    loss_xc[xc_me] = ordered(loss_y, 8)
-    xc_copies = [rem_copy(loss_xc.at[xc_me], loss_xc.at[xc_me], xc_send.at[i], xc_recv.at[i], dev)
-                 for i, dev in enumerate(xc_devs)]
-    for c in xc_copies:
-        c.start()
     to_ext.wait_recv()
     to_sum.wait_recv()
     grad_text_ref[...] = factor * (
         grad_text_ref[...] + ext_in[...].astype(jnp.float32) + sum_in[...].astype(jnp.float32))
-    for c in xc_copies:
+    for c in y_copies:
         c.wait_recv()
-    whole = jnp.sum(jnp.sum(ordered(loss_xc, 8), axis=1, keepdims=True), axis=0, keepdims=True)
+    whole = jnp.sum(jnp.sum(ordered(loss_y, 8), axis=1, keepdims=True), axis=0, keepdims=True)
     loss_ref[...] = whole / (blocks * 2 * rows)
 
     for c in [text_1, to_mate, to_ext, to_sum] + over + back + xc_copies + y_copies + z_copies:

time: 62.1 us -> 58 us (0.934)
  Pallas kernels: 60 us -> 55.5 us
    pallas_call x1, Pallas kernels: 58.3 us -> 53.8 us  [body(): pl.pallas_call(kernel, out_shape=(jax.ShapeDtypeStruct((1, 1), jnp.float3...]
where the time goes in v6:
time: 58 us; the launch traced here: 57.4 us
  Pallas kernels  55.5 us (96%)
  between operations  1.93 us (3%)
    pallas_call x1, Pallas kernels, body(): pl.pallas_call(kernel, out_shape=(jax.ShapeDtypeStruct((1, 1), jnp.float3...  53.8 us
    pallas_call x1, Pallas kernels, body(): pl.pallas_call(hand_over, out_shape=(jax.ShapeDtypeStruct((1, 1), jnp.flo...  1.67 us

profile of v6, /device:TPU:1, one launch (start us, length us, event | category | flops | bytes accessed | tf_op | source)
XLA Modules:
  0.0 57.4 jit_solution(8429592682735251243)
XLA Ops:
  1.9 53.8 %band.1 = (f32[1,1]{1,0:T(1,128)}, f32[128,1152]{1,0:T(8,128)S(1)}, f32[128,1152]{1,0:T(8,128)S(1)}) custom-call(bf16[128,1152]{1,0:T(8,128)(2,1)} %image_hbm.1, bf16[128,1152]{1,0:T(8,128)(2,1)} %text_hbm.1, s32[2,128]{1,0:T(2,128)} %bitcast.2, f32[1]{0:T(128)S(6)} %copy.8.scale_ref, f32[1]{0:T(128)S(6)} %copy.9.bias_ref), custom_call_target="tpu_custom_call" | custom-call | flops 905969664 | bytes 1179648 | tf_op jit(solution)/shard_map/band/pallas_call | solution.py:363
  55.8 1.7 %hand_over.1 = (f32[1,1]{1,0:T(1,128)}, f32[128,1152]{1,0:T(8,128)}, f32[128,1152]{1,0:T(8,128)}) custom-call(f32[1,1]{1,0:T(1,128)} %get-tuple-element.9.loss_in, f32[128,1152]{1,0:T(8,128)S(1)} %get-tuple-element.10.image_in, f32[128,1152]{1,0:T(8,128)S(1)} %get-tuple-element.11.text_in), custom_call_target="tpu_custom_call" | custom-call | tf_op jit(solution)/shard_map/hand_over/pallas_call | solution.py:388

commit v7 on v6

--- a/solution.py
+++ b/solution.py
@@ -45,7 +45,7 @@
     mate = (b + 1 - 2 * core, g)
     xc_me = x * 2 + core
     xc_peers = [lax.rem(xc_me + i, 8) for i in range(1, 8)]
-    y_peers = [lax.rem(y + i, 8) for i in range(1, 8)]
+    y_peers = [lax.rem(y + i, 8) for i in (4, 3, 5, 2, 6, 1, 7)]
     r_peers = [lax.rem(zr + i, 4) for i in range(1, 4)]
     q_peers = [lax.rem(zq + i, 3) for i in range(1, 3)]
     xc_devs = [place(p // 2, y, z, p % 2) for p in xc_peers]

time: 58 us -> 57.8 us (level)
  no operation moved by 1% of the time
where the time goes in v7:
time: 57.8 us; the launch traced here: 57.6 us
  Pallas kernels  55.7 us (96%)
  between operations  1.93 us (3%)
    pallas_call x1, Pallas kernels, body(): pl.pallas_call(kernel, out_shape=(jax.ShapeDtypeStruct((1, 1), jnp.float3...  54 us
    pallas_call x1, Pallas kernels, body(): pl.pallas_call(hand_over, out_shape=(jax.ShapeDtypeStruct((1, 1), jnp.flo...  1.67 us

profile of v7, /device:TPU:1, one launch (start us, length us, event | category | flops | bytes accessed | tf_op | source)
XLA Modules:
  0.0 57.6 jit_solution(6281173057553302742)
XLA Ops:
  1.9 54.0 %band.1 = (f32[1,1]{1,0:T(1,128)}, f32[128,1152]{1,0:T(8,128)S(1)}, f32[128,1152]{1,0:T(8,128)S(1)}) custom-call(bf16[128,1152]{1,0:T(8,128)(2,1)} %image_hbm.1, bf16[128,1152]{1,0:T(8,128)(2,1)} %text_hbm.1, s32[2,128]{1,0:T(2,128)} %bitcast.2, f32[1]{0:T(128)S(6)} %copy.8.scale_ref, f32[1]{0:T(128)S(6)} %copy.9.bias_ref), custom_call_target="tpu_custom_call" | custom-call | flops 905969664 | bytes 1179648 | tf_op jit(solution)/shard_map/band/pallas_call | solution.py:363
  55.9 1.7 %hand_over.1 = (f32[1,1]{1,0:T(1,128)}, f32[128,1152]{1,0:T(8,128)}, f32[128,1152]{1,0:T(8,128)}) custom-call(f32[1,1]{1,0:T(1,128)} %get-tuple-element.9.loss_in, f32[128,1152]{1,0:T(8,128)S(1)} %get-tuple-element.10.image_in, f32[128,1152]{1,0:T(8,128)S(1)} %get-tuple-element.11.text_in), custom_call_target="tpu_custom_call" | custom-call | tf_op jit(solution)/shard_map/hand_over/pallas_call | solution.py:388
